TPU v7x, 32 devices: a whole 2x2x4 slice. The times are simulated.
32 devices in a mesh: seq: 8 (over z, x), doc: 4 (over y, core).
Axes of the slice: x: 2, y: 2, z: 4, core: 2. Of those that a mesh axis runs over, the one named last changes fastest.
Arguments:
- values: bfloat16 [4, 2048, 4096], P('doc', 'seq'), may hold values from -6 to 6
- b_in: bfloat16 [4, 2048, 128], P('doc', 'seq'), may hold values from -0.032958984 to 0.032958984
- c_in: bfloat16 [4, 2048, 128], P('doc', 'seq'), may hold values from -6 to 6
- log_decay: float32 [4, 64, 2048], P('doc', None, 'seq'), may hold values from -1 to 0, as said below
- skip: float32 [64], replicated, may hold values from 0.5 to 1.5
- owner: int32 [4, 16], P(None, 'seq'), may hold values from -1 to 3, as said below
Outputs:
- owned: bfloat16 [4, 64, 128, 4096], P('doc', 'seq')
Inputs may be any that keep to these rules, and one draw needn't show every extreme that they name: `log_decay`: all entries are at most 0. In each head the per-token rates vary from token to token and from shard to shard. Within each shard of 2 blocks of a document, both blocks name the same owner (so no block is marked -1); in general -1 marks a block that is not kept.
All inputs are finite; a program needn't handle non-finite values.
Results may differ from a plain program's by a relative error of at most 0.0063.
Values may be sent and summed in bfloat16 or wider, within the bound.
A program may use at most 192 MiB of HBM per device.

v0:
```python
import functools

import jax
import jax.numpy as jnp
from jax import lax
from jax.experimental import pallas as pl
from jax.experimental.pallas import tpu as pltpu
from jax.sharding import PartitionSpec as P

Q = 128
CAP = 2
MESH = pl.DeviceIdType.MESH
F32 = jnp.float32
BF16 = jnp.bfloat16


def layer_kernel(
    n_seq, n_doc, heads, width, chunks, group,
    v_hbm, b_hbm, c_hbm, ld_hbm, skip_hbm, gathered,
    v_buf, b_ref, c_ref, ld_ref, skip_ref, lhs_buf, sb_buf, a_buf, d_buf, row_buf, l_buf, x_out, x_in, p_out, p_in, e_out, e_in, o_buf,
    in_sem, own_sem, xs, xr, ps, pr, es, e2s, er, ys, yr, cs, cr, fs, fr,
):
    seq_len, row_width = v_buf.shape
    blocks = seq_len // Q
    state_dim = b_ref.shape[1]
    head_dim = row_width // heads
    sides = n_doc // 2
    rungs = n_seq // 2
    seq = lax.axis_index("seq")
    doc = lax.axis_index("doc")
    rung, second = seq // 2, seq % 2
    side, core = doc // 2, doc % 2
    across = (seq + 1 - 2 * second, doc)
    above = (seq + 2, doc)
    below = (seq - 2, doc)
    above2 = (seq + 4, doc)
    below2 = (seq - 4, doc)
    odd = rung % 2 == 1
    has_above = rung < rungs - 1
    sends_p = jnp.logical_not(odd) & has_above
    sends_e = odd & has_above
    sends_e2 = odd & (rung < rungs - 2)
    takes_e = rung > 1
    from_below2 = odd & takes_e
    twin = (seq, doc + 1 - 2 * core)
    far = [(seq, ((side + j) % sides) * 2 + core) for j in range(1, sides)]

    pairs = [(ld_hbm, ld_ref), (skip_hbm, skip_ref), (b_hbm, b_ref), (c_hbm, c_ref), (v_hbm, v_buf)]
    loads = [pltpu.make_async_copy(a, b, in_sem.at[i]) for i, (a, b) in enumerate(pairs)]
    for load in loads:
        load.start()

    barrier = pltpu.get_barrier_semaphore()
    for other in [across, twin] + far:
        pl.semaphore_signal(barrier, inc=1, device_id=other, device_id_type=MESH)

    @pl.when(rung > 0)
    def _():
        pl.semaphore_signal(barrier, inc=1, device_id=below, device_id_type=MESH)

    @pl.when(has_above)
    def _():
        pl.semaphore_signal(barrier, inc=1, device_id=above, device_id_type=MESH)

    @pl.when(sends_e2)
    def _():
        pl.semaphore_signal(barrier, inc=1, device_id=above2, device_id_type=MESH)

    @pl.when(from_below2)
    def _():
        pl.semaphore_signal(barrier, inc=1, device_id=below2, device_id_type=MESH)

    for load in loads[:-1]:
        load.wait()

    rows_i = lax.broadcasted_iota(jnp.int32, (Q, Q), 0)
    cols_i = lax.broadcasted_iota(jnp.int32, (Q, Q), 1)
    lower = rows_i >= cols_i
    ones_lower = jnp.where(lower, 1.0, 0.0).astype(F32)
    lane = lax.broadcasted_iota(jnp.int32, (1, 2 * heads), 1)
    twice = (
        lax.broadcasted_iota(jnp.int32, (heads, 2 * heads), 1) % heads
        == lax.broadcasted_iota(jnp.int32, (heads, 2 * heads), 0)
    )
    skip_row = jnp.dot(
        jnp.broadcast_to(skip_ref[...], (8, heads)), jnp.where(twice, 1.0, 0.0).astype(F32),
        precision=lax.Precision.HIGHEST, preferred_element_type=F32,
    )[0:1]

    def split(x):
        high = x.astype(BF16).astype(F32)
        return jnp.where(lane < heads, high, x - high).astype(BF16)

    small = [skip_row]
    halves, totals, befores = [], [], []
    running = jnp.zeros((1, 2 * heads), F32)
    for k in range(blocks):
        span = slice(k * Q, (k + 1) * Q)
        decay = ld_ref[:, span]
        decay = jnp.concatenate([decay, decay], axis=0)
        cum = lax.dot_general(
            ones_lower, decay, (((1,), (1,)), ((), ())),
            precision=lax.Precision.HIGHEST, preferred_element_type=F32,
        )
        total = cum[Q - 1:Q]
        half = 0.5 * total
        lhs_buf[2 * k * Q:(2 * k + 1) * Q, :] = split(jnp.exp(cum - half))
        lhs_buf[(2 * k + 1) * Q:(2 * k + 2) * Q, :] = split(jnp.exp(half - cum))
        running = running + total
        halves.append(jnp.exp(half))
        totals.append(jnp.exp(total))
        befores.append(jnp.exp(running))
        b_block = b_ref[span, :]
        scores = lax.dot_general(
            c_ref[span, :], b_block, (((1,), (1,)), ((), ())), preferred_element_type=F32
        )
        sb_buf[k, 0:Q, :] = jnp.where(lower, scores, 0.0).astype(BF16)
        sb_buf[k, Q:Q + state_dim, :] = b_block.astype(F32).T.astype(BF16)
    small = [skip_row] + halves + totals + befores
    row_count = row_buf.shape[1]
    row_id = lax.broadcasted_iota(jnp.int32, (row_count, 2 * heads), 0)
    stacked = jnp.zeros((row_count, 2 * heads), F32)
    for i, row in enumerate(small):
        stacked = jnp.where(row_id == i, row, stacked)
    base = 2 * blocks * Q
    lhs_buf[base:base + row_count, :] = split(stacked)

    @pl.when(jnp.logical_not(takes_e))
    def _():
        e_in[...] = jnp.zeros_like(e_in)

    @pl.when(jnp.logical_not(odd))
    def _():
        p_in[...] = jnp.zeros_like(p_in)

    peers = 2 + len(far) + jnp.where(rung > 0, 1, 0) + jnp.where(has_above, 1, 0)
    peers = peers + jnp.where(sends_e2, 1, 0) + jnp.where(from_below2, 1, 0)
    pl.semaphore_wait(barrier, peers)
    loads[-1].wait()

    def x_copy(g):
        return pltpu.make_async_remote_copy(
            x_out.at[g], x_in.at[g], xs.at[g], xr.at[g], device_id=across, device_id_type=MESH)

    def p_copy(g):
        return pltpu.make_async_remote_copy(
            p_out.at[g], p_in.at[g], ps.at[g], pr.at[g], device_id=above, device_id_type=MESH)

    def e_copy(g):
        return pltpu.make_async_remote_copy(
            e_out.at[g], e_in.at[g], es.at[g], er.at[g], device_id=above, device_id_type=MESH)

    def e2_copy(g):
        return pltpu.make_async_remote_copy(
            e_out.at[g], e_in.at[g], e2s.at[g], er.at[g], device_id=above2, device_id_type=MESH)

    def with_decay(buf, g, state, decay):
        high = decay.astype(BF16).astype(F32)
        tail = lax.broadcasted_iota(jnp.int32, (16, width), 0)
        buf[g, 0:state_dim, :] = state.astype(BF16)
        buf[g, state_dim:state_dim + 16, :] = jnp.where(
            tail == 0, high, jnp.where(tail == 1, decay - high, 0.0)).astype(BF16)

    def without_decay(buf, g):
        tail = buf[g, state_dim:state_dim + 16, :].astype(F32)
        return buf[g, 0:state_dim, :].astype(F32), tail[0:1] + tail[1:2]

    def far_copy(j, g):
        return pltpu.make_async_remote_copy(
            o_buf.at[g], gathered.at[doc, g], ys.at[j, g], yr.at[j, g],
            device_id=far[j], device_id_type=MESH)

    def twin_copy(g):
        return pltpu.make_async_remote_copy(
            o_buf.at[g], gathered.at[doc, g], cs.at[g], cr.at[g],
            device_id=twin, device_id_type=MESH)

    def own_copy(g):
        return pltpu.make_async_copy(o_buf.at[g], gathered.at[doc, g], own_sem.at[g])

    def forward_copy(j, g):
        source = ((side + sides - 1 - j) % sides) * 2 + core
        return pltpu.make_async_remote_copy(
            gathered.at[source, g], gathered.at[source, g], fs.at[j, g], fr.at[j, g],
            device_id=twin, device_id_type=MESH)

    def local_part(g, carry):
        lanes = pl.ds(pl.multiple_of(g * width, width), width)
        head_of = lax.broadcasted_iota(jnp.int32, (2 * heads, width), 1) // head_dim
        head_at = lax.broadcasted_iota(jnp.int32, (2 * heads, width), 0) % heads
        spread = jnp.where(head_at == head_of + g * (width // head_dim), 1.0, 0.0).astype(BF16)
        rows = jnp.dot(lhs_buf[base:base + row_count, :], spread, preferred_element_type=F32)
        row_buf[g] = rows
        state = jnp.zeros((state_dim, width), F32)
        for k in range(blocks):
            a_buf[g, k * Q:(k + 1) * Q, :] = jnp.dot(
                lhs_buf[2 * k * Q:(2 * k + 1) * Q, :], spread, preferred_element_type=F32)
            grow = jnp.dot(
                lhs_buf[(2 * k + 1) * Q:(2 * k + 2) * Q, :], spread, preferred_element_type=F32)
            scaled = (v_buf[k * Q:(k + 1) * Q, lanes].astype(F32) * grow).astype(BF16)
            both = jnp.dot(sb_buf[k], scaled, preferred_element_type=F32)
            d_buf[g, k * Q:(k + 1) * Q, :] = both[0:Q]
            state = rows[1 + blocks + k:2 + blocks + k] * state + rows[1 + k:2 + k] * both[Q:]
            l_buf[k, g] = state
        with_decay(x_out, g, state, rows[3 * blocks:3 * blocks + 1])
        x_copy(g).start()
        return carry

    ahead = min(2, chunks // group)
    lax.fori_loop(0, ahead * group, local_part, 0)

    def carried_part(step, part):
        g = step * group + part
        lanes = pl.ds(pl.multiple_of(g * width, width), width)
        o_lanes = pl.ds(part * width, width)
        rows = row_buf[g]
        x_copy(g).wait_recv()
        other, other_decay = without_decay(x_in, g)
        mine = l_buf[blocks - 1, g]
        mine_decay = rows[3 * blocks:3 * blocks + 1]
        is_second = second == 1
        first_state = jnp.where(is_second, other, mine)
        last_state = jnp.where(is_second, mine, other)
        first_decay = jnp.where(is_second, other_decay, mine_decay)
        last_decay = jnp.where(is_second, mine_decay, other_decay)

        @pl.when(sends_p)
        def _():
            with_decay(p_out, g, last_decay * first_state + last_state, first_decay * last_decay)
            p_copy(g).start()

        @pl.when(odd)
        def _():
            p_copy(g).wait_recv()

        @pl.when(takes_e)
        def _():
            e_copy(g).wait_recv()

        past = e_in[g].astype(F32)
        under, under_decay = without_decay(p_in, g)
        enter = jnp.where(odd, under_decay * past + under, past)
        middle = first_decay * enter + first_state

        @pl.when(sends_e)
        def _():
            e_out[g] = (last_decay * middle + last_state).astype(BF16)

        @pl.when(sends_e2)
        def _():
            e2_copy(g).start()

        @pl.when(sends_e)
        def _():
            e_copy(g).start()

        enter = jnp.where(is_second, middle, enter)
        skip_lanes = rows[0:1]
        for k in range(blocks):
            span = slice(k * Q, (k + 1) * Q)
            at_block = enter
            if k > 0:
                at_block = rows[2 * blocks + k:2 * blocks + k + 1] * enter + l_buf[k - 1, g]
            scaled = (rows[1 + k:2 + k] * at_block).astype(BF16)
            inner = d_buf[g, span, :] + jnp.dot(
                c_ref[span, :], scaled, preferred_element_type=F32)
            o_buf[g // group, span, o_lanes] = (
                a_buf[g, span, :] * inner + skip_lanes * v_buf[span, lanes].astype(F32)
            ).astype(BF16)

    def send(step):
        for j in range(len(far)):
            far_copy(j, step).start()
        twin_copy(step).start()
        own_copy(step).start()

    def outputs(step, carry):
        for part in range(group):
            carried_part(step, part)
        send(step)
        return carry

    def outputs_and_later(step, carry):
        outputs(step, carry)
        for part in range(group):
            local_part((step + ahead) * group + part, carry)
        return carry

    steps = chunks // group
    lax.fori_loop(0, steps - ahead, outputs_and_later, 0)
    lax.fori_loop(steps - ahead, steps, outputs, 0)

    def forward(g, carry):
        for j in range(len(far)):
            far_copy(j, g).wait_recv()
            forward_copy(j, g).start()
        return carry

    lax.fori_loop(0, steps, forward, 0)

    def finish(g, carry):
        for j in range(len(far)):
            far_copy(j, g).wait_send()
            forward_copy(j, g).wait()
        twin_copy(g).wait()
        own_copy(g).wait()
        return carry

    lax.fori_loop(0, steps, finish, 0)

    def finish_states(g, carry):
        x_copy(g).wait_send()

        @pl.when(sends_p)
        def _():
            p_copy(g).wait_send()

        @pl.when(sends_e)
        def _():
            e_copy(g).wait_send()

        @pl.when(sends_e2)
        def _():
            e2_copy(g).wait_send()

        return carry

    lax.fori_loop(0, chunks, finish_states, 0)


def pick_kernel(blocks, owner, me, taken, out, zeros, held, flat, load_sem, store_sem):
    chunks, width = taken.shape[1], taken.shape[3]
    slots = out.shape[1]
    places = []
    for i in range(slots):
        doc, rank = i // CAP, i % CAP
        seen = jnp.int32(0)
        block = jnp.int32(0)
        present = jnp.bool_(False)
        for j in range(blocks):
            match = owner[j, doc] == me[0]
            hit = match & (seen == rank)
            block = jnp.where(hit, j, block)
            present = present | hit
            seen = seen + match.astype(jnp.int32)
        places.append(present)
        rows = pl.ds(pl.multiple_of(block * Q, Q), Q)

        @pl.when(present)
        def _():
            pltpu.make_async_copy(
                taken.at[doc, :, rows, :], held.at[i], load_sem.at[i]
            ).start()

    zeros[...] = jnp.zeros_like(zeros)
    for i, present in enumerate(places):

        @pl.when(jnp.logical_not(present))
        def _():
            pltpu.make_async_copy(zeros, out.at[0, i], store_sem.at[i]).start()

    for i, present in enumerate(places):

        @pl.when(present)
        def _():
            pltpu.make_async_copy(held.at[i], held.at[i], load_sem.at[i]).wait()

            def relay(g, carry):
                flat[i, :, pl.ds(pl.multiple_of(g * width, width), width)] = held[i, g]
                return carry

            lax.fori_loop(0, chunks, relay, 0)
            pltpu.make_async_copy(flat.at[i], out.at[0, i], store_sem.at[i]).start()

    for i in range(slots):
        pltpu.make_async_copy(zeros, out.at[0, i], store_sem.at[i]).wait()


def local(n_seq, n_doc, values, b_in, c_in, log_decay, skip, owner):
    seq_len, row_width = values.shape[1], values.shape[2]
    heads = log_decay.shape[1]
    state_dim = b_in.shape[2]
    blocks = seq_len // Q
    group = 2
    width = 128
    chunks = row_width // width
    steps, step_width = chunks // group, width * group
    far = n_doc // 2 - 1
    row_count = -(-(1 + 3 * blocks) // 16) * 16
    smem = pl.BlockSpec(memory_space=pltpu.SMEM)
    anywhere = pl.BlockSpec(memory_space=pl.ANY)
    dma = pltpu.SemaphoreType.DMA
    gathered = pl.pallas_call(
        functools.partial(layer_kernel, n_seq, n_doc, heads, width, chunks, group),
        out_shape=jax.ShapeDtypeStruct((n_doc, steps, seq_len, step_width), BF16),
        in_specs=[anywhere] * 5,
        out_specs=anywhere,
        scratch_shapes=[
            pltpu.VMEM((seq_len, row_width), BF16),
            pltpu.VMEM((seq_len, state_dim), BF16),
            pltpu.VMEM((seq_len, state_dim), BF16),
            pltpu.VMEM((heads, seq_len), F32),
            pltpu.VMEM((1, heads), F32),
            pltpu.VMEM((2 * seq_len + row_count, 2 * heads), BF16),
            pltpu.VMEM((blocks, Q + state_dim, Q), BF16),
            pltpu.VMEM((chunks, seq_len, width), F32),
            pltpu.VMEM((chunks, seq_len, width), F32),
            pltpu.VMEM((chunks, row_count, width), F32),
            pltpu.VMEM((blocks, chunks, state_dim, width), F32),
            pltpu.VMEM((chunks, state_dim + 16, width), BF16),
            pltpu.VMEM((chunks, state_dim + 16, width), BF16),
            pltpu.VMEM((chunks, state_dim + 16, width), BF16),
            pltpu.VMEM((chunks, state_dim + 16, width), BF16),
            pltpu.VMEM((chunks, state_dim, width), BF16),
            pltpu.VMEM((chunks, state_dim, width), BF16),
            pltpu.VMEM((steps, seq_len, step_width), BF16),
            dma((5,)),
            dma((steps,)),
            dma((chunks,)),
            dma((chunks,)),
            dma((chunks,)),
            dma((chunks,)),
            dma((chunks,)),
            dma((chunks,)),
            dma((chunks,)),
            dma((far, steps)),
            dma((far, steps)),
            dma((steps,)),
            dma((steps,)),
            dma((far, steps)),
            dma((far, steps)),
        ],
        compiler_params=pltpu.CompilerParams(
            collective_id=0, has_side_effects=True, vmem_limit_bytes=60 * 2**20
        ),
        name="layer",
    )(values[0], b_in[0], c_in[0], log_decay[0], skip.reshape(1, heads))

    slots = n_doc * CAP
    me = lax.axis_index("doc").astype(jnp.int32).reshape(1)

    return pl.pallas_call(
        functools.partial(pick_kernel, blocks),
        out_shape=jax.ShapeDtypeStruct((1, slots, Q, row_width), BF16),
        in_specs=[smem, smem, anywhere],
        out_specs=anywhere,
        scratch_shapes=[
            pltpu.VMEM((Q, row_width), BF16),
            pltpu.VMEM((slots, steps, Q, step_width), BF16),
            pltpu.VMEM((slots, Q, row_width), BF16),
            dma((slots,)),
            dma((slots,)),
        ],
        compiler_params=pltpu.CompilerParams(vmem_limit_bytes=60 * 2**20),
        name="pick",
    )(owner.T, me, gathered)


def solution(mesh):
    in_specs = (
        P("doc", "seq", None),
        P("doc", "seq", None),
        P("doc", "seq", None),
        P("doc", None, "seq"),
        P(),
        P(None, "seq"),
    )
    out_specs = P("doc", "seq", None, None)
    body = functools.partial(local, mesh.shape["seq"], mesh.shape["doc"])
    return jax.shard_map(body, mesh=mesh, in_specs=in_specs, out_specs=out_specs, check_vma=False)
```

profile of v0, /device:TPU:25, one launch (start us, length us, event | category | flops | bytes accessed | tf_op | source)
XLA Modules:
  0.0 75.1 jit_solution(12579001796532762003)
XLA Ops:
  0.0 70.0 %layer.1.taken = bf16[4,16,256,256]{3,2,1,0:T(8,128)(2,1)} custom-call(bf16[256,4096]{1,0:T(8,128)(2,1)} %bitcast.7, bf16[256,128]{1,0:T(8,128)(2,1)} %bitcast.8, bf16[256,128]{1,0:T(8,128)(2,1)} %bitcast.9, f32[64,256]{1,0:T(8,128)} %bitcast.10, f32[1,64]{1,0:T(1,128)} %bitcast.12), custom_call_target="tpu_custom_call" | custom-call | tf_op jit(solution)/shard_map/layer/pallas_call | solution.py:393
  70.0 5.1 %pick.1 = bf16[1,8,128,4096]{3,2,1,0:T(8,128)(2,1)} custom-call(s32[2,4]{1,0:T(2,128)} %bitcast.11, s32[1]{0:T(128)} %bitcast.1.me, bf16[4,16,256,256]{3,2,1,0:T(8,128)(2,1)} %layer.1.taken), custom_call_target="tpu_custom_call" | custom-call | tf_op jit(solution)/shard_map/pick/pallas_call | solution.py:442
where the time goes:
time: 75.3 us; the launch traced here: 75.1 us
  Pallas kernels  75.1 us (100%)
    pallas_call x1, Pallas kernels, local(): pl.pallas_call(functools.partial(layer_kernel, n_seq, n_doc, heads, width...  70 us
    pallas_call x1, Pallas kernels, local(): pl.pallas_call(functools.partial(pick_kernel, blocks), out_shape=jax.Shap...  5.07 us

commit v1 on v0

--- a/solution.py
+++ b/solution.py
@@ -36,6 +36,7 @@
     above2 = (seq + 4, doc)
     below2 = (seq - 4, doc)
     odd = rung % 2 == 1
+    head_start = p_in.shape[0]
     has_above = rung < rungs - 1
     sends_p = jnp.logical_not(odd) & has_above
     sends_e = odd & has_above
@@ -125,9 +126,13 @@
     base = 2 * blocks * Q
     lhs_buf[base:base + row_count, :] = split(stacked)
 
-    @pl.when(jnp.logical_not(takes_e))
+    @pl.when(rung == 0)
     def _():
         e_in[...] = jnp.zeros_like(e_in)
+
+    @pl.when(rung == 1)
+    def _():
+        e_in[0:head_start] = jnp.zeros((head_start, state_dim, width), BF16)
 
     @pl.when(jnp.logical_not(odd))
     def _():
@@ -209,7 +214,7 @@
     ahead = min(2, chunks // group)
     lax.fori_loop(0, ahead * group, local_part, 0)
 
-    def carried_part(step, part):
+    def carried_part(step, part, early):
         g = step * group + part
         lanes = pl.ds(pl.multiple_of(g * width, width), width)
         o_lanes = pl.ds(part * width, width)
@@ -224,33 +229,42 @@
         first_decay = jnp.where(is_second, other_decay, mine_decay)
         last_decay = jnp.where(is_second, mine_decay, other_decay)
 
-        @pl.when(sends_p)
-        def _():
-            with_decay(p_out, g, last_decay * first_state + last_state, first_decay * last_decay)
-            p_copy(g).start()
-
-        @pl.when(odd)
-        def _():
-            p_copy(g).wait_recv()
-
-        @pl.when(takes_e)
+        if early:
+
+            @pl.when(sends_p)
+            def _():
+                pair_state = last_decay * first_state + last_state
+                with_decay(p_out, g, pair_state, first_decay * last_decay)
+                p_copy(g).start()
+
+        if early:
+
+            @pl.when(odd)
+            def _():
+                p_copy(g).wait_recv()
+
+        @pl.when(takes_e if early else rung > 0)
         def _():
             e_copy(g).wait_recv()
 
-        past = e_in[g].astype(F32)
-        under, under_decay = without_decay(p_in, g)
-        enter = jnp.where(odd, under_decay * past + under, past)
+        enter = e_in[g].astype(F32)
+        if early:
+            under, under_decay = without_decay(p_in, g)
+            enter = jnp.where(odd, under_decay * enter + under, enter)
         middle = first_decay * enter + first_state
-
-        @pl.when(sends_e)
+        sends = sends_e if early else has_above
+
+        @pl.when(sends)
         def _():
             e_out[g] = (last_decay * middle + last_state).astype(BF16)
 
-        @pl.when(sends_e2)
-        def _():
-            e2_copy(g).start()
-
-        @pl.when(sends_e)
+        if early:
+
+            @pl.when(sends_e2)
+            def _():
+                e2_copy(g).start()
+
+        @pl.when(sends)
         def _():
             e_copy(g).start()
 
@@ -274,21 +288,23 @@
         twin_copy(step).start()
         own_copy(step).start()
 
-    def outputs(step, carry):
+    def outputs(early, step, carry):
         for part in range(group):
-            carried_part(step, part)
+            carried_part(step, part, early)
         send(step)
         return carry
 
-    def outputs_and_later(step, carry):
-        outputs(step, carry)
+    def outputs_and_later(early, step, carry):
+        outputs(early, step, carry)
         for part in range(group):
             local_part((step + ahead) * group + part, carry)
         return carry
 
     steps = chunks // group
-    lax.fori_loop(0, steps - ahead, outputs_and_later, 0)
-    lax.fori_loop(steps - ahead, steps, outputs, 0)
+    first = head_start // group
+    lax.fori_loop(0, first, functools.partial(outputs_and_later, True), 0)
+    lax.fori_loop(first, steps - ahead, functools.partial(outputs_and_later, False), 0)
+    lax.fori_loop(steps - ahead, steps, functools.partial(outputs, False), 0)
 
     def forward(g, carry):
         for j in range(len(far)):
@@ -310,7 +326,11 @@
 
     def finish_states(g, carry):
         x_copy(g).wait_send()
-
+        return carry
+
+    lax.fori_loop(0, chunks, finish_states, 0)
+
+    def finish_first(g, carry):
         @pl.when(sends_p)
         def _():
             p_copy(g).wait_send()
@@ -325,7 +345,16 @@
 
         return carry
 
-    lax.fori_loop(0, chunks, finish_states, 0)
+    lax.fori_loop(0, head_start, finish_first, 0)
+
+    def finish_chain(g, carry):
+        @pl.when(has_above)
+        def _():
+            e_copy(g).wait_send()
+
+        return carry
+
+    lax.fori_loop(head_start, chunks, finish_chain, 0)
 
 
 def pick_kernel(blocks, owner, me, taken, out, zeros, held, flat, load_sem, store_sem):
@@ -385,6 +414,7 @@
     width = 128
     chunks = row_width // width
     steps, step_width = chunks // group, width * group
+    head_start = min(2, steps - 2) * group
     far = n_doc // 2 - 1
     row_count = -(-(1 + 3 * blocks) // 16) * 16
     smem = pl.BlockSpec(memory_space=pltpu.SMEM)
@@ -409,8 +439,8 @@
             pltpu.VMEM((blocks, chunks, state_dim, width), F32),
             pltpu.VMEM((chunks, state_dim + 16, width), BF16),
             pltpu.VMEM((chunks, state_dim + 16, width), BF16),
-            pltpu.VMEM((chunks, state_dim + 16, width), BF16),
-            pltpu.VMEM((chunks, state_dim + 16, width), BF16),
+            pltpu.VMEM((head_start, state_dim + 16, width), BF16),
+            pltpu.VMEM((head_start, state_dim + 16, width), BF16),
             pltpu.VMEM((chunks, state_dim, width), BF16),
             pltpu.VMEM((chunks, state_dim, width), BF16),
             pltpu.VMEM((steps, seq_len, step_width), BF16),

time: 75.3 us -> 72.3 us (0.960)
  Pallas kernels: 75.1 us -> 71.5 us
    pallas_call x1, Pallas kernels: 70 us -> 65.4 us  [local(): pl.pallas_call(functools.partial(layer_kernel, n_seq, n_doc, heads, width...]
    pallas_call x1, Pallas kernels: 5.07 us -> 6.1 us  [local(): pl.pallas_call(functools.partial(pick_kernel, blocks), out_shape=jax.Shap...]
where the time goes in v1:
time: 72.3 us; the launch traced here: 71.5 us
  Pallas kernels  71.5 us (99%)
    pallas_call x1, Pallas kernels, local(): pl.pallas_call(functools.partial(layer_kernel, n_seq, n_doc, heads, width...  65.4 us
    pallas_call x1, Pallas kernels, local(): pl.pallas_call(functools.partial(pick_kernel, blocks), out_shape=jax.Shap...  6.1 us

profile of v1, /device:TPU:25, one launch (start us, length us, event | category | flops | bytes accessed | tf_op | source)
XLA Modules:
  0.0 71.5 jit_solution(14093429111648945905)
XLA Ops:
  0.0 65.4 %layer.1.taken = bf16[4,16,256,256]{3,2,1,0:T(8,128)(2,1)} custom-call(bf16[256,4096]{1,0:T(8,128)(2,1)} %bitcast.7, bf16[256,128]{1,0:T(8,128)(2,1)} %bitcast.8, bf16[256,128]{1,0:T(8,128)(2,1)} %bitcast.9, f32[64,256]{1,0:T(8,128)} %bitcast.10, f32[1,64]{1,0:T(1,128)} %bitcast.12), custom_call_target="tpu_custom_call" | custom-call | tf_op jit(solution)/shard_map/layer/pallas_call | solution.py:423
  65.4 6.1 %pick.1 = bf16[1,8,128,4096]{3,2,1,0:T(8,128)(2,1)} custom-call(s32[2,4]{1,0:T(2,128)} %bitcast.11, s32[1]{0:T(128)} %bitcast.1.me, bf16[4,16,256,256]{3,2,1,0:T(8,128)(2,1)} %layer.1.taken), custom_call_target="tpu_custom_call" | custom-call | tf_op jit(solution)/shard_map/pick/pallas_call | solution.py:472
